TPU v7x, 256 devices: a whole 4x4x8 slice. The times are simulated.
256 devices in a mesh: seq: 64 (over y_lo, z, x), pipe: 4 (over y_hi, core).
Axes of the slice: x: 4, y: 4 (y_hi: 2, y_lo: 2; y = y_hi * 2 + y_lo), z: 8, core: 2. Of those that a mesh axis runs over, the one named last changes fastest.
Arguments:
- noisy_q: bfloat16 [4, 4096, 8192], P('pipe', 'seq'), may hold values from -8 to 8
- noisy_k: bfloat16 [4, 4096, 1024], P('pipe', 'seq'), may hold values from -8 to 8
- noisy_v: bfloat16 [4, 4096, 1024], P('pipe', 'seq'), may hold values from -6 to 6
- clean_k: bfloat16 [4, 4096, 1024], P('pipe', 'seq'), may hold values from -6 to 6
- clean_v: bfloat16 [4, 4096, 1024], P('pipe', 'seq'), may hold values from -6 to 6
- noisy_o: bfloat16 [4, 4096, 8192], P('pipe', 'seq'), may hold values from -6 to 6
- out_grad: bfloat16 [4, 4096, 8192], P('pipe', 'seq'), may hold values from -6 to 6
- block_mask: int32 [4, 32, 32], P('pipe'), may hold values 0 or 1
Outputs:
- passed_grad: bfloat16 [4, 4096, 8192], P('pipe', 'seq')
- noisy_k_grad: bfloat16 [4, 4096, 1024], P('pipe', 'seq')
- noisy_v_grad: bfloat16 [4, 4096, 1024], P('pipe', 'seq')
- clean_k_grad: bfloat16 [4, 4096, 1024], P('pipe', 'seq')
- clean_v_grad: bfloat16 [4, 4096, 1024], P('pipe', 'seq')
All inputs are finite; a program needn't handle non-finite values. No bound on the sum of `block_mask` on one device may be relied on, other than what follows from the above.
Results may differ from a plain program's by a relative error of at most 0.0058.
Values may be sent and summed in bfloat16 or wider, within the bound.
A program may use at most 128 MiB of HBM per device.

v0:
```python
import jax
import jax.numpy as jnp
from jax import lax
from jax.sharding import PartitionSpec as P

HEAD_FEATURES = 128
BLOCK = 128
WINDOW = 4


def passed_along(block, axis, distance):
    devices = range(lax.axis_size(axis))
    route = [((i - distance) % len(devices), i) for i in devices]
    return lax.ppermute(block, axis, route)


def attend_heads(queries, grads, keys_n, values_n, keys_c, values_c, row_delta, mask_rows):
    length = queries.shape[0]
    head_count = queries.shape[1]
    nblock = length // BLOCK
    logit_scale = HEAD_FEATURES ** (-0.5)
    block_shape = (nblock, BLOCK, head_count, HEAD_FEATURES)
    query_blk = queries.reshape(block_shape)
    grad_blk = grads.reshape(block_shape)
    key_blk = keys_n.reshape(block_shape)
    value_blk = values_n.reshape(block_shape)

    def windowed(blocks):
        empty = jnp.zeros((WINDOW,) + blocks.shape[1:], blocks.dtype)
        padded = jnp.concatenate([empty, blocks], axis=0)
        return jnp.concatenate([padded[slot : slot + nblock] for slot in range(WINDOW)], axis=1)

    key_win = windowed(keys_c.reshape(block_shape))
    value_win = windowed(values_c.reshape(block_shape))
    block_ids = jnp.arange(nblock, dtype=jnp.int32)
    source = block_ids[:, None] - WINDOW + jnp.arange(WINDOW, dtype=jnp.int32)[None, :]
    hits = (block_ids[None, None, :] == source[:, :, None]) & (mask_rows[:, None, :] == 1)
    seen = jnp.any(hits, axis=-1)
    seen_keys = jnp.repeat(seen, BLOCK, axis=1)
    noisy_scores = (
        jnp.einsum("bqhd,bkhd->bhqk", query_blk, key_blk, preferred_element_type=jnp.float32)
        * logit_scale
    )
    clean_scores = (
        jnp.einsum("bqhd,bkhd->bhqk", query_blk, key_win, preferred_element_type=jnp.float32)
        * logit_scale
    )
    clean_scores = jnp.where(seen_keys[:, None, None, :], clean_scores, jnp.float32(-1e30))
    row_top = jnp.maximum(noisy_scores.max(-1), clean_scores.max(-1))
    row_total = jnp.exp(noisy_scores - row_top[..., None]).sum(-1) + jnp.exp(
        clean_scores - row_top[..., None]
    ).sum(-1)
    row_lse = row_top + jnp.log(row_total)
    delta_blk = row_delta.reshape(nblock, BLOCK, head_count).transpose(0, 2, 1)
    probs_n = jnp.exp(noisy_scores - row_lse[..., None])
    probs_c = jnp.exp(clean_scores - row_lse[..., None])
    noisy_prob_gradient = jnp.einsum(
        "bqhd,bkhd->bhqk", grad_blk, value_blk, preferred_element_type=jnp.float32
    )
    noisy_score_gradient = (probs_n * (noisy_prob_gradient - delta_blk[..., None])).astype(
        jnp.bfloat16
    )
    clean_prob_gradient = jnp.einsum(
        "bqhd,bkhd->bhqk", grad_blk, value_win, preferred_element_type=jnp.float32
    )
    clean_score_gradient = (probs_c * (clean_prob_gradient - delta_blk[..., None])).astype(
        jnp.bfloat16
    )
    dquery_acc = jnp.einsum(
        "bhqk,bkhd->bqhd", noisy_score_gradient, key_blk, preferred_element_type=jnp.float32
    )
    dquery_acc = dquery_acc + jnp.einsum(
        "bhqk,bkhd->bqhd", clean_score_gradient, key_win, preferred_element_type=jnp.float32
    )
    query_gradient = (
        (logit_scale * dquery_acc).astype(jnp.bfloat16).reshape(length, head_count, HEAD_FEATURES)
    )
    dkey_noisy = (
        logit_scale
        * jnp.einsum(
            "bhqk,bqhd->bkhd", noisy_score_gradient, query_blk, preferred_element_type=jnp.float32
        )
    ).astype(jnp.bfloat16)
    dvalue_noisy = jnp.einsum(
        "bhqk,bqhd->bkhd",
        probs_n.astype(jnp.bfloat16),
        grad_blk,
        preferred_element_type=jnp.float32,
    ).astype(jnp.bfloat16)
    dkey_window = logit_scale * jnp.einsum(
        "bhqk,bqhd->bkhd", clean_score_gradient, query_blk, preferred_element_type=jnp.float32
    )
    dvalue_window = jnp.einsum(
        "bhqk,bqhd->bkhd",
        probs_c.astype(jnp.bfloat16),
        grad_blk,
        preferred_element_type=jnp.float32,
    )

    def unwind(window_terms):
        slots = window_terms.reshape(nblock, WINDOW, BLOCK, head_count, HEAD_FEATURES)
        summed = jnp.zeros((nblock + WINDOW, BLOCK, head_count, HEAD_FEATURES), jnp.float32)
        for slot in range(WINDOW):
            summed = summed + jnp.pad(
                slots[:, slot], ((slot, WINDOW - slot), (0, 0), (0, 0), (0, 0))
            )
        return summed[WINDOW:].reshape(length, head_count, HEAD_FEATURES).astype(jnp.bfloat16)

    dkey_clean = unwind(dkey_window)
    dvalue_clean = unwind(dvalue_window)
    dkey_noisy = dkey_noisy.reshape(length, head_count, HEAD_FEATURES)
    dvalue_noisy = dvalue_noisy.reshape(length, head_count, HEAD_FEATURES)
    return (
        query_gradient[None],
        dkey_noisy[None],
        dvalue_noisy[None],
        dkey_clean[None],
        dvalue_clean[None],
    )


def per_device(noisy_q, noisy_k, noisy_v, clean_k, clean_v, noisy_o, out_grad, block_mask):
    tokens = noisy_q.shape[1]
    head_count = noisy_q.shape[2] // HEAD_FEATURES
    kv_count = noisy_k.shape[2] // HEAD_FEATURES
    group_size = head_count // kv_count
    query_four = noisy_q.reshape(1, tokens, head_count, HEAD_FEATURES)
    saved_four = noisy_o.reshape(1, tokens, head_count, HEAD_FEATURES)
    grad_four = out_grad.reshape(1, tokens, head_count, HEAD_FEATURES)

    def widen(array):
        return jnp.repeat(array.reshape(1, tokens, kv_count, HEAD_FEATURES), group_size, axis=2)

    key_nw, value_nw, key_cw, value_cw = (
        widen(noisy_k),
        widen(noisy_v),
        widen(clean_k),
        widen(clean_v),
    )
    q_in, o_in, g_in, kn_in, vn_in, kc_in, vc_in = (
        lax.all_to_all(query_four, "seq", split_axis=2, concat_axis=1, tiled=True),
        lax.all_to_all(saved_four, "seq", split_axis=2, concat_axis=1, tiled=True),
        lax.all_to_all(grad_four, "seq", split_axis=2, concat_axis=1, tiled=True),
        lax.all_to_all(key_nw, "seq", split_axis=2, concat_axis=1, tiled=True),
        lax.all_to_all(value_nw, "seq", split_axis=2, concat_axis=1, tiled=True),
        lax.all_to_all(key_cw, "seq", split_axis=2, concat_axis=1, tiled=True),
        lax.all_to_all(value_cw, "seq", split_axis=2, concat_axis=1, tiled=True),
    )
    row_delta = jnp.sum(g_in[0].astype(jnp.float32) * o_in[0].astype(jnp.float32), axis=2)
    query_gradient, dkey_noisy, dvalue_noisy, dkey_clean, dvalue_clean = attend_heads(
        q_in[0], g_in[0], kn_in[0], vn_in[0], kc_in[0], vc_in[0], row_delta, block_mask[0]
    )
    q_back, kn_back, vn_back, kc_back, vc_back = (
        lax.all_to_all(query_gradient, "seq", split_axis=1, concat_axis=2, tiled=True),
        lax.all_to_all(dkey_noisy, "seq", split_axis=1, concat_axis=2, tiled=True),
        lax.all_to_all(dvalue_noisy, "seq", split_axis=1, concat_axis=2, tiled=True),
        lax.all_to_all(dkey_clean, "seq", split_axis=1, concat_axis=2, tiled=True),
        lax.all_to_all(dvalue_clean, "seq", split_axis=1, concat_axis=2, tiled=True),
    )
    passed_grad = q_back.reshape(1, tokens, head_count * HEAD_FEATURES)
    passed_grad = passed_along(passed_grad, "pipe", -1)

    def fold_groups(per_head):
        summed = (
            per_head.reshape(1, tokens, kv_count, group_size, HEAD_FEATURES)
            .astype(jnp.float32)
            .sum(3)
        )
        return summed.astype(jnp.bfloat16).reshape(1, tokens, kv_count * HEAD_FEATURES)

    return (
        passed_grad,
        fold_groups(kn_back),
        fold_groups(vn_back),
        fold_groups(kc_back),
        fold_groups(vc_back),
    )


def solution(mesh):
    in_specs = (
        P("pipe", "seq", None),
        P("pipe", "seq", None),
        P("pipe", "seq", None),
        P("pipe", "seq", None),
        P("pipe", "seq", None),
        P("pipe", "seq", None),
        P("pipe", "seq", None),
        P("pipe", None, None),
    )
    out_specs = (
        P("pipe", "seq", None),
        P("pipe", "seq", None),
        P("pipe", "seq", None),
        P("pipe", "seq", None),
        P("pipe", "seq", None),
    )
    return jax.shard_map(
        per_device, mesh=mesh, in_specs=in_specs, out_specs=out_specs, check_vma=False
    )
```

profile of v0, /device:TPU:16, one launch (start us, length us, event | category | flops | bytes accessed | tf_op | source)
XLA Modules:
  0.0 572.0 jit_solution(486031536509071705)
XLA Ops:
  0.7 1.2 copy-done
  1.9 1.3 copy_bitcast_fusion.2
  3.1 12.7 %all-to-all-start = ((bf16[1,64,64,128]{3,1,0,2:T(8,128)(2,1)}), bf16[1,64,64,128]{3,1,0,2:T(8,128)(2,1)S(1)}, u32[]{:S(2)}, u32[]{:S(2)}) async-start(bf16[1,64,64,128]{3,1,0,2:T(8,128)(2,1)} %copy_bitcast_fusion.2), calls=%async_computation | async-start | bytes 2097152 | tf_op jit(solution)/shard_map/all_to_all | solution.py:141
  15.9 28.0 %all-to-all-done = bf16[1,64,64,128]{3,1,0,2:T(8,128)(2,1)S(1)} async-done(((bf16[1,64,64,128]{3,1,0,2:T(8,128)(2,1)}), bf16[1,64,64,128]{3,1,0,2:T(8,128)(2,1)S(1)}, u32[]{:S(2)}, u32[]{:S(2)}) %all-to-all-start) | async-done | bytes 1048608 | tf_op jit(solution)/shard_map/all_to_all | solution.py:141
  43.9 1.4 broadcast_in_dim.47
  45.3 6.6 %all-to-all-start.1 = ((bf16[1,64,64,128]{3,1,0,2:T(8,128)(2,1)}), bf16[1,64,64,128]{3,1,0,2:T(8,128)(2,1)S(1)}, u32[]{:S(2)}, u32[]{:S(2)}) async-start(bf16[1,64,64,128]{3,1,0,2:T(8,128)(2,1)} %bitcast.3), calls=%async_computation.1 | async-start | bytes 2097152 | tf_op jit(solution)/shard_map/all_to_all | solution.py:144
  51.9 1.3 copy_bitcast_fusion.1
  53.2 25.9 %all-to-all-done.1 = bf16[1,64,64,128]{3,1,0,2:T(8,128)(2,1)S(1)} async-done(((bf16[1,64,64,128]{3,1,0,2:T(8,128)(2,1)}), bf16[1,64,64,128]{3,1,0,2:T(8,128)(2,1)S(1)}, u32[]{:S(2)}, u32[]{:S(2)}) %all-to-all-start.1) | async-done | bytes 1048608 | tf_op jit(solution)/shard_map/all_to_all | solution.py:144
  79.1 6.6 %all-to-all-start.3 = ((bf16[1,64,64,128]{3,1,0,2:T(8,128)(2,1)}), bf16[1,64,64,128]{3,1,0,2:T(8,128)(2,1)S(1)}, u32[]{:S(2)}, u32[]{:S(2)}) async-start(bf16[1,64,64,128]{3,1,0,2:T(8,128)(2,1)} %copy_bitcast_fusion.1), calls=%async_computation.3 | async-start | bytes 2097152 | tf_op jit(solution)/shard_map/all_to_all | solution.py:143
  85.8 2.6 copy_bitcast_fusion
  88.3 24.3 %all-to-all-done.3 = bf16[1,64,64,128]{3,1,0,2:T(8,128)(2,1)S(1)} async-done(((bf16[1,64,64,128]{3,1,0,2:T(8,128)(2,1)}), bf16[1,64,64,128]{3,1,0,2:T(8,128)(2,1)S(1)}, u32[]{:S(2)}, u32[]{:S(2)}) %all-to-all-start.3) | async-done | bytes 1048608 | tf_op jit(solution)/shard_map/all_to_all | solution.py:143
  112.7 6.6 %all-to-all-start.5 = ((bf16[1,64,64,128]{3,1,0,2:T(8,128)(2,1)}), bf16[1,64,64,128]{3,1,0,2:T(8,128)(2,1)S(1)}, u32[]{:S(2)}, u32[]{:S(2)}) async-start(bf16[1,64,64,128]{3,1,0,2:T(8,128)(2,1)} %copy_bitcast_fusion), calls=%async_computation.5 | async-start | bytes 2097152 | tf_op jit(solution)/shard_map/all_to_all | solution.py:142
  119.4 26.7 %all-to-all-done.5 = bf16[1,64,64,128]{3,1,0,2:T(8,128)(2,1)S(1)} async-done(((bf16[1,64,64,128]{3,1,0,2:T(8,128)(2,1)}), bf16[1,64,64,128]{3,1,0,2:T(8,128)(2,1)S(1)}, u32[]{:S(2)}, u32[]{:S(2)}) %all-to-all-start.5) | async-done | bytes 1048608 | tf_op jit(solution)/shard_map/all_to_all | solution.py:142
  146.1 1.3 broadcast_in_dim.52
  147.4 6.6 %all-to-all-start.2 = ((bf16[1,64,64,128]{3,1,0,2:T(8,128)(2,1)}), bf16[1,64,64,128]{3,1,0,2:T(8,128)(2,1)S(1)}, u32[]{:S(2)}, u32[]{:S(2)}) async-start(bf16[1,64,64,128]{3,1,0,2:T(8,128)(2,1)} %bitcast.277), calls=%async_computation.2 | async-start | bytes 2097152 | tf_op jit(solution)/shard_map/all_to_all | solution.py:146
  154.1 26.6 %all-to-all-done.2 = bf16[1,64,64,128]{3,1,0,2:T(8,128)(2,1)S(1)} async-done(((bf16[1,64,64,128]{3,1,0,2:T(8,128)(2,1)}), bf16[1,64,64,128]{3,1,0,2:T(8,128)(2,1)S(1)}, u32[]{:S(2)}, u32[]{:S(2)}) %all-to-all-start.2) | async-done | bytes 1048608 | tf_op jit(solution)/shard_map/all_to_all | solution.py:146
  180.8 1.3 broadcast_in_dim.55
  182.1 6.5 %all-to-all-start.4 = ((bf16[1,64,64,128]{3,1,0,2:T(8,128)(2,1)}), bf16[1,64,64,128]{3,1,0,2:T(8,128)(2,1)S(1)}, u32[]{:S(2)}, u32[]{:S(2)}) async-start(bf16[1,64,64,128]{3,1,0,2:T(8,128)(2,1)} %bitcast.276), calls=%async_computation.4 | async-start | bytes 2097152 | tf_op jit(solution)/shard_map/all_to_all | solution.py:145
  189.1 1.8 fusion.21
  191.1 3.0 pad_slice_fusion.7
  196.0 5.2 bitcast_reduce_fusion
  201.2 14.0 %all-to-all-done.4 = bf16[1,64,64,128]{3,1,0,2:T(8,128)(2,1)S(1)} async-done(((bf16[1,64,64,128]{3,1,0,2:T(8,128)(2,1)}), bf16[1,64,64,128]{3,1,0,2:T(8,128)(2,1)S(1)}, u32[]{:S(2)}, u32[]{:S(2)}) %all-to-all-start.4) | async-done | bytes 1048608 | tf_op jit(solution)/shard_map/all_to_all | solution.py:145
  215.3 1.3 broadcast_in_dim.57
  216.6 6.5 %all-to-all-start.6 = ((bf16[1,64,64,128]{3,1,0,2:T(8,128)(2,1)}), bf16[1,64,64,128]{3,1,0,2:T(8,128)(2,1)}, u32[]{:S(2)}, u32[]{:S(2)}) async-start(bf16[1,64,64,128]{3,1,0,2:T(8,128)(2,1)} %bitcast.28), calls=%async_computation.6 | async-start | bytes 2097152 | tf_op jit(solution)/shard_map/all_to_all | solution.py:147
  223.1 2.4 multiply_reduce_fusion
  225.9 7.1 %fusion.2 = f32[32,128]{1,0:T(8,128)S(1)} fusion(f32[32,512,128]{2,1,0:T(8,128)} %get-tuple-element.24, f32[32,128]{1,0:T(8,128)S(1)} %max.13, pred[32,512]{1,0:T(8,128)(4,1)S(1)} %bitcast.285), kind=kLoop, calls=%fused_computation.6 | loop fusion | flops 8384512 | bytes 8437760 | tf_op jit(solution)/shard_map/reduce_sum | solution.py:52
  234.9 1.9 fusion.38
  236.8 12.7 %all-to-all-done.6 = bf16[1,64,64,128]{3,1,0,2:T(8,128)(2,1)} async-done(((bf16[1,64,64,128]{3,1,0,2:T(8,128)(2,1)}), bf16[1,64,64,128]{3,1,0,2:T(8,128)(2,1)}, u32[]{:S(2)}, u32[]{:S(2)}) %all-to-all-start.6) | async-done | bytes 1048608 | tf_op jit(solution)/shard_map/all_to_all | solution.py:147
  249.5 3.0 pad_slice_fusion.3
  252.4 6.0 %fusion = bf16[32,128,512]{1,2,0:T(8,128)(2,1)S(1)} fusion(f32[32,512,128]{2,1,0:T(8,128)} %get-tuple-element.24, f32[32,128]{1,0:T(8,128)S(1)} %sub.70, f32[32,128]{1,0:T(8,128)S(1)} %log_add_fusion, pred[32,512]{1,0:T(8,128)(4,1)S(1)} %bitcast.286, bf16[32,128,128]{2,1,0:T(8,128)(2,1)S(1)} %bitcast.246, ...), kind=kOutput, calls=%fused_computation.1 | convolution fusion | flops 566231040 | bytes 17874944 | tf_op jit(solution)/shard_map/bqhd,bkhd->bhqk/dot_general | solution.py:63
  258.5 6.3 %fusion.23 = bf16[32,128,128]{1,2,0:T(8,128)(2,1)} fusion(f32[32,128,128]{2,1,0:T(8,128)S(1)} %copy-done.12, bf16[32,128,512]{1,2,0:T(8,128)(2,1)S(1)} %fusion, bf16[32,128,1,128]{3,1,0,2:T(8,128)(2,1)} %copy-done.16, bf16[32,128,1,128]{3,1,0,2:T(8,128)(2,1)} %copy-done.15, bf16[32,128,1,128]{3,1,0,2:T(8,128)(2,1)} %copy-done.14, ...), kind=kOutput, calls=%fused_computation.46 | convolution fusion | flops 555220992 | bytes 11534336 | tf_op jit(solution)/shard_map/bhqk,bkhd->bqhd/dot_general | solution.py:72
  264.7 4.3 copy.202
  269.6 24.4 %reduce.18 = bf16[4096,128]{1,0:T(8,128)(2,1)} reduce(bf16[4096,1,1,128]{3,2,1,0:T(2,128)(2,1)} %bitcast.261, bf16[]{:T(256)} %broadcast.103), dimensions={1,2}, to_apply=%bitcast.243.reduce_sub_computation | reduce | bytes 2097154
  294.0 2.1 reshape.351
  296.1 6.5 %all-to-all-start.7 = ((bf16[64,2,4096]{2,1,0:T(2,128)(2,1)}), bf16[64,2,4096]{2,1,0:T(2,128)(2,1)}, u32[]{:S(2)}, u32[]{:S(2)}) async-start(bf16[64,2,4096]{2,1,0:T(2,128)(2,1)} %reshape.351), calls=%async_computation.7 | async-start | bytes 2097152 | tf_op jit(solution)/shard_map/all_to_all | solution.py:154
  302.7 3.5 fusion.25
  306.1 2.3 copy.146
  308.4 4.3 copy.201
  312.7 24.4 %reduce.19 = bf16[4096,128]{1,0:T(8,128)(2,1)} reduce(bf16[4096,1,1,128]{3,2,1,0:T(2,128)(2,1)} %bitcast.263, bf16[]{:T(256)} %broadcast.103), dimensions={1,2}, to_apply=%bitcast.242.reduce_sub_computation | reduce | bytes 2097154
  337.1 2.1 reshape.353
  339.3 11.9 %all-to-all-start.8 = ((bf16[64,2,4096]{2,1,0:T(2,128)(2,1)}), bf16[64,2,4096]{2,1,0:T(2,128)(2,1)}, u32[]{:S(2)}, u32[]{:S(2)}) async-start(bf16[64,2,4096]{2,1,0:T(2,128)(2,1)} %reshape.353), calls=%async_computation.8 | async-start | bytes 2097152 | tf_op jit(solution)/shard_map/all_to_all | solution.py:155
  351.7 16.7 %copy.200 = bf16[1,4096,1,128]{3,2,0,1:T(2,128)(2,1)S(1)} copy(bf16[1,4096,1,128]{3,1,2,0:T(8,128)(2,1)S(1)} %bitcast.278) | data formatting | bytes 2097152 | tf_op jit(solution)/shard_map/broadcast_in_dim;reshape | solution.py:116
  368.5 23.4 %reduce.20 = bf16[4096,128]{1,0:T(8,128)(2,1)} reduce(bf16[4096,1,1,128]{3,2,1,0:T(2,128)(2,1)S(1)} %bitcast.264, bf16[]{:T(256)} %broadcast.103), dimensions={1,2}, to_apply=%bitcast.241.reduce_sub_computation | reduce | bytes 2097154
  391.8 2.2 reshape.355
  394.1 12.1 %all-to-all-start.9 = ((bf16[64,2,4096]{2,1,0:T(2,128)(2,1)}), bf16[64,2,4096]{2,1,0:T(2,128)(2,1)}, u32[]{:S(2)}, u32[]{:S(2)}) async-start(bf16[64,2,4096]{2,1,0:T(2,128)(2,1)} %reshape.355), calls=%async_computation.9 | async-start | bytes 2097152 | tf_op jit(solution)/shard_map/all_to_all | solution.py:156
  406.2 3.4 broadcast_multiply_fusion
  411.5 16.7 %copy.199 = bf16[1,4096,1,128]{3,2,0,1:T(2,128)(2,1)S(1)} copy(bf16[1,4096,1,128]{3,1,2,0:T(8,128)(2,1)S(1)} %bitcast.266) | data formatting | bytes 2097152 | tf_op jit(solution)/shard_map/convert_element_type | solution.py:107
  428.3 23.4 %reduce.21 = bf16[4096,128]{1,0:T(8,128)(2,1)} reduce(bf16[4096,1,1,128]{3,2,1,0:T(2,128)(2,1)S(1)} %bitcast.265, bf16[]{:T(256)} %broadcast.103), dimensions={1,2}, to_apply=%bitcast.240.reduce_sub_computation | reduce | bytes 2097154
  451.7 2.1 reshape.357
  453.8 11.8 %all-to-all-start.10 = ((bf16[64,2,4096]{2,1,0:T(2,128)(2,1)}), bf16[64,2,4096]{2,1,0:T(2,128)(2,1)}, u32[]{:S(2)}, u32[]{:S(2)}) async-start(bf16[64,2,4096]{2,1,0:T(2,128)(2,1)} %reshape.357), calls=%async_computation.10 | async-start | bytes 2097152 | tf_op jit(solution)/shard_map/all_to_all | solution.py:157
  465.6 7.5 %fusion.5 = f32[32,512,128]{2,1,0:T(8,128)S(1)} fusion(bf16[32,128,128]{2,1,0:T(8,128)(2,1)S(1)} %bitcast.248, f32[32,512,128]{2,1,0:T(8,128)} %get-tuple-element.24, f32[32,128]{1,0:T(8,128)S(1)} %log_add_fusion, pred[32,512]{1,0:T(8,128)(4,1)S(1)} %bitcast.287), kind=kOutput, calls=%fused_computation.10 | convolution fusion | flops 545259520 | bytes 17858560 | tf_op jit(solution)/shard_map/bhqk,bqhd->bkhd/dot_general | solution.py:93
  475.1 16.7 %copy.198 = bf16[1,4096,1,128]{3,2,0,1:T(2,128)(2,1)S(1)} copy(bf16[1,4096,1,128]{3,1,2,0:T(8,128)(2,1)S(1)} %bitcast.267) | data formatting | bytes 2097152 | tf_op jit(solution)/shard_map/convert_element_type | solution.py:107
  491.8 22.4 %reduce.22 = bf16[4096,128]{1,0:T(8,128)(2,1)S(1)} reduce(bf16[4096,1,1,128]{3,2,1,0:T(2,128)(2,1)S(1)} %bitcast.262, bf16[]{:T(256)} %broadcast.103), dimensions={1,2}, to_apply=%bitcast.239.reduce_sub_computation | reduce | bytes 2097154
  515.4 11.4 %all-to-all-start.11 = ((bf16[64,2,4096]{2,1,0:T(2,128)(2,1)}), bf16[64,2,4096]{2,1,0:T(2,128)(2,1)S(1)}, u32[]{:S(2)}, u32[]{:S(2)}) async-start(bf16[64,2,4096]{2,1,0:T(2,128)(2,1)} %reshape.359), calls=%async_computation.11 | async-start | bytes 2097152 | tf_op jit(solution)/shard_map/all_to_all | solution.py:158
  526.8 6.5 %reshape.352 = bf16[4096,1,1,128]{3,2,1,0:T(2,128)(2,1)S(1)} reshape(bf16[64,2,4096]{2,1,0:T(2,128)(2,1)} %all-to-all-done.7) | data formatting | bytes 2097152
  534.1 1.3 reshape.339
  535.6 6.5 %reshape.354 = bf16[4096,1,1,128]{3,2,1,0:T(2,128)(2,1)S(1)} reshape(bf16[64,2,4096]{2,1,0:T(2,128)(2,1)} %all-to-all-done.8) | data formatting | bytes 2097152
  543.2 1.4 reduce_sum.78
  545.4 6.5 %reshape.356 = bf16[4096,1,1,128]{3,2,1,0:T(2,128)(2,1)S(1)} reshape(bf16[64,2,4096]{2,1,0:T(2,128)(2,1)} %all-to-all-done.9) | data formatting | bytes 2097152
  553.0 1.4 reduce_sum.79
  555.3 6.5 %reshape.358 = bf16[4096,1,1,128]{3,2,1,0:T(2,128)(2,1)S(1)} reshape(bf16[64,2,4096]{2,1,0:T(2,128)(2,1)} %all-to-all-done.10) | data formatting | bytes 2097152
  562.9 1.4 reduce_sum.80
  567.3 1.4 reduce_sum.81
  569.5 2.3 copy.204
  (94 shorter events, 20.7 us)
Async XLA Ops:
  0.6 1.2 copy-start
  0.6 15.2 %copy-start.18 = (bf16[1,64,1024]{2,1,0:T(8,128)(2,1)S(1)}, bf16[1,64,1024]{2,1,0:T(8,128)(2,1)}, u32[]{:S(2)}) copy-start(bf16[1,64,1024]{2,1,0:T(8,128)(2,1)} %param.9) | copy-start | bytes 393220
  3.1 40.8 %all-to-all-start = ((bf16[1,64,64,128]{3,1,0,2:T(8,128)(2,1)}), bf16[1,64,64,128]{3,1,0,2:T(8,128)(2,1)S(1)}, u32[]{:S(2)}, u32[]{:S(2)}) async-start(bf16[1,64,64,128]{3,1,0,2:T(8,128)(2,1)} %copy_bitcast_fusion.2), calls=%async_computation | async-start | bytes 2097152 | tf_op jit(solution)/shard_map/all_to_all | solution.py:141
  15.8 36.1 %copy-start.17 = (bf16[1,64,8192]{2,1,0:T(8,128)(2,1)S(1)}, bf16[1,64,8192]{2,1,0:T(8,128)(2,1)}, u32[]{:S(2)}) copy-start(bf16[1,64,8192]{2,1,0:T(8,128)(2,1)} %param.14) | copy-start | bytes 3145732
  43.9 150.2 %copy-start.2 = (bf16[1,64,64,128]{3,1,0,2:T(8,128)(2,1)}, bf16[1,64,64,128]{3,1,0,2:T(8,128)(2,1)S(1)}, u32[]{:S(2)}) copy-start(bf16[1,64,64,128]{3,1,0,2:T(8,128)(2,1)S(1)} %all-to-all-done) | copy-start | bytes 3145732
  45.3 33.8 %all-to-all-start.1 = ((bf16[1,64,64,128]{3,1,0,2:T(8,128)(2,1)}), bf16[1,64,64,128]{3,1,0,2:T(8,128)(2,1)S(1)}, u32[]{:S(2)}, u32[]{:S(2)}) async-start(bf16[1,64,64,128]{3,1,0,2:T(8,128)(2,1)} %bitcast.3), calls=%async_computation.1 | async-start | bytes 2097152 | tf_op jit(solution)/shard_map/all_to_all | solution.py:144
  79.1 9.2 %copy-start.5 = (bf16[1,64,64,128]{3,1,0,2:T(8,128)(2,1)}, bf16[1,64,64,128]{3,1,0,2:T(8,128)(2,1)S(1)}, u32[]{:S(2)}) copy-start(bf16[1,64,64,128]{3,1,0,2:T(8,128)(2,1)S(1)} %all-to-all-done.1) | copy-start | bytes 3145732
  79.1 33.6 %all-to-all-start.3 = ((bf16[1,64,64,128]{3,1,0,2:T(8,128)(2,1)}), bf16[1,64,64,128]{3,1,0,2:T(8,128)(2,1)S(1)}, u32[]{:S(2)}, u32[]{:S(2)}) async-start(bf16[1,64,64,128]{3,1,0,2:T(8,128)(2,1)} %copy_bitcast_fusion.1), calls=%async_computation.3 | async-start | bytes 2097152 | tf_op jit(solution)/shard_map/all_to_all | solution.py:143
  85.7 33.6 %copy-start.19 = (bf16[1,64,1024]{2,1,0:T(8,128)(2,1)S(1)}, bf16[1,64,1024]{2,1,0:T(8,128)(2,1)}, u32[]{:S(2)}) copy-start(bf16[1,64,1024]{2,1,0:T(8,128)(2,1)} %param.11) | copy-start | bytes 393220
  112.7 33.4 %all-to-all-start.5 = ((bf16[1,64,64,128]{3,1,0,2:T(8,128)(2,1)}), bf16[1,64,64,128]{3,1,0,2:T(8,128)(2,1)S(1)}, u32[]{:S(2)}, u32[]{:S(2)}) async-start(bf16[1,64,64,128]{3,1,0,2:T(8,128)(2,1)} %copy_bitcast_fusion), calls=%async_computation.5 | async-start | bytes 2097152 | tf_op jit(solution)/shard_map/all_to_all | solution.py:142
  119.3 34.7 %copy-start.20 = (bf16[1,64,1024]{2,1,0:T(8,128)(2,1)S(1)}, bf16[1,64,1024]{2,1,0:T(8,128)(2,1)}, u32[]{:S(2)}) copy-start(bf16[1,64,1024]{2,1,0:T(8,128)(2,1)} %param.10) | copy-start | bytes 393220
  146.1 1.3 copy-start.11
  147.4 33.4 %all-to-all-start.2 = ((bf16[1,64,64,128]{3,1,0,2:T(8,128)(2,1)}), bf16[1,64,64,128]{3,1,0,2:T(8,128)(2,1)S(1)}, u32[]{:S(2)}, u32[]{:S(2)}) async-start(bf16[1,64,64,128]{3,1,0,2:T(8,128)(2,1)} %bitcast.277), calls=%async_computation.2 | async-start | bytes 2097152 | tf_op jit(solution)/shard_map/all_to_all | solution.py:146
  154.0 34.6 %copy-start.22 = (s32[1,32,32]{2,1,0:T(8,128)S(1)}, s32[1,32,32]{2,1,0:T(8,128)}, u32[]{:S(2)}) copy-start(s32[1,32,32]{2,1,0:T(8,128)} %param.15) | copy-start | bytes 12292
  154.0 35.1 %copy-start.21 = (bf16[1,64,1024]{2,1,0:T(8,128)(2,1)S(1)}, bf16[1,64,1024]{2,1,0:T(8,128)(2,1)}, u32[]{:S(2)}) copy-start(bf16[1,64,1024]{2,1,0:T(8,128)(2,1)} %param.12) | copy-start | bytes 393220
  180.8 1.3 copy-start.9
  182.1 33.2 %all-to-all-start.4 = ((bf16[1,64,64,128]{3,1,0,2:T(8,128)(2,1)}), bf16[1,64,64,128]{3,1,0,2:T(8,128)(2,1)S(1)}, u32[]{:S(2)}, u32[]{:S(2)}) async-start(bf16[1,64,64,128]{3,1,0,2:T(8,128)(2,1)} %bitcast.276), calls=%async_computation.4 | async-start | bytes 2097152 | tf_op jit(solution)/shard_map/all_to_all | solution.py:145
  194.0 1.0 copy-start.13
  194.0 1.3 copy-start.14
  194.1 1.6 copy-start.15
  194.1 2.0 copy-start.16
  215.3 7.8 %copy-start.7 = (bf16[1,64,64,128]{3,1,0,2:T(8,128)(2,1)}, bf16[1,64,64,128]{3,1,0,2:T(8,128)(2,1)S(1)}, u32[]{:S(2)}) copy-start(bf16[1,64,64,128]{3,1,0,2:T(8,128)(2,1)S(1)} %all-to-all-done.4) | copy-start | bytes 3145732
  216.6 32.9 %all-to-all-start.6 = ((bf16[1,64,64,128]{3,1,0,2:T(8,128)(2,1)}), bf16[1,64,64,128]{3,1,0,2:T(8,128)(2,1)}, u32[]{:S(2)}, u32[]{:S(2)}) async-start(bf16[1,64,64,128]{3,1,0,2:T(8,128)(2,1)} %bitcast.28), calls=%async_computation.6 | async-start | bytes 2097152 | tf_op jit(solution)/shard_map/all_to_all | solution.py:147
  225.9 7.1 %copy-start.8 = (bf16[1,64,64,128]{3,1,0,2:T(8,128)(2,1)S(1)}, bf16[1,64,64,128]{3,1,0,2:T(8,128)(2,1)}, u32[]{:S(2)}) copy-start(bf16[1,64,64,128]{3,1,0,2:T(8,128)(2,1)} %copy-done.7) | copy-start | bytes 3145732
  233.0 1.9 copy-start.6
  233.9 1.0 copy-start.4
  252.4 6.0 %copy-start.12 = (f32[32,128,128]{2,1,0:T(8,128)S(1)}, f32[32,128,128]{2,1,0:T(8,128)}, u32[]{:S(2)}) copy-start(f32[32,128,128]{2,1,0:T(8,128)} %fusion.38) | copy-start | bytes 6291460
  258.5 6.3 %copy-start.10 = (bf16[32,128,512]{1,2,0:T(8,128)(2,1)}, bf16[32,128,512]{1,2,0:T(8,128)(2,1)S(1)}, u32[]{:S(2)}) copy-start(bf16[32,128,512]{1,2,0:T(8,128)(2,1)S(1)} %fusion) | copy-start | bytes 12582916
  296.1 43.2 %all-to-all-start.7 = ((bf16[64,2,4096]{2,1,0:T(2,128)(2,1)}), bf16[64,2,4096]{2,1,0:T(2,128)(2,1)}, u32[]{:S(2)}, u32[]{:S(2)}) async-start(bf16[64,2,4096]{2,1,0:T(2,128)(2,1)} %reshape.351), calls=%async_computation.7 | async-start | bytes 2097152 | tf_op jit(solution)/shard_map/all_to_all | solution.py:154
  339.3 54.8 %all-to-all-start.8 = ((bf16[64,2,4096]{2,1,0:T(2,128)(2,1)}), bf16[64,2,4096]{2,1,0:T(2,128)(2,1)}, u32[]{:S(2)}, u32[]{:S(2)}) async-start(bf16[64,2,4096]{2,1,0:T(2,128)(2,1)} %reshape.353), calls=%async_computation.8 | async-start | bytes 2097152 | tf_op jit(solution)/shard_map/all_to_all | solution.py:155
  391.8 14.4 %copy-start.3 = (bf16[1,64,64,128]{3,1,0,2:T(8,128)(2,1)S(1)}, bf16[1,64,64,128]{3,1,0,2:T(8,128)(2,1)}, u32[]{:S(2)}) copy-start(bf16[1,64,64,128]{3,1,0,2:T(8,128)(2,1)} %copy-done.2) | copy-start | bytes 3145732
  394.1 59.7 %all-to-all-start.9 = ((bf16[64,2,4096]{2,1,0:T(2,128)(2,1)}), bf16[64,2,4096]{2,1,0:T(2,128)(2,1)}, u32[]{:S(2)}, u32[]{:S(2)}) async-start(bf16[64,2,4096]{2,1,0:T(2,128)(2,1)} %reshape.355), calls=%async_computation.9 | async-start | bytes 2097152 | tf_op jit(solution)/shard_map/all_to_all | solution.py:156
  453.8 61.6 %all-to-all-start.10 = ((bf16[64,2,4096]{2,1,0:T(2,128)(2,1)}), bf16[64,2,4096]{2,1,0:T(2,128)(2,1)}, u32[]{:S(2)}, u32[]{:S(2)}) async-start(bf16[64,2,4096]{2,1,0:T(2,128)(2,1)} %reshape.357), calls=%async_computation.10 | async-start | bytes 2097152 | tf_op jit(solution)/shard_map/all_to_all | solution.py:157
  515.4 49.7 %all-to-all-start.11 = ((bf16[64,2,4096]{2,1,0:T(2,128)(2,1)}), bf16[64,2,4096]{2,1,0:T(2,128)(2,1)S(1)}, u32[]{:S(2)}, u32[]{:S(2)}) async-start(bf16[64,2,4096]{2,1,0:T(2,128)(2,1)} %reshape.359), calls=%async_computation.11 | async-start | bytes 2097152 | tf_op jit(solution)/shard_map/all_to_all | solution.py:158
  535.4 34.1 %collective-permute-start = (bf16[1,64,8192]{2,1,0:T(8,128)(2,1)}, bf16[1,64,8192]{2,1,0:T(8,128)(2,1)}, u32[]{:S(2)}, u32[]{:S(2)}) collective-permute-start(bf16[1,64,8192]{2,1,0:T(8,128)(2,1)} %reshape.339), channel_id=1, source_target_pairs={{1,0},{2,1},{3,2},{0,3},{5,4},{6,5},{7,6},{4,7},{9,8},{10,9},{11,1... | collective-permute-start | bytes 3145736 | tf_op jit(solution)/shard_map/ppermute | solution.py:14
  566.1 5.7 copy-start.1
where the time goes:
time: 584 us; the launch traced here: 572 us
  waiting for transfers between devices  158 us (27%)
  other arithmetic  135 us (23%)
  local copies, waits for them, and re-layouts  134 us (23%)
  starting transfers between devices  106 us (18%)
  matrix products  37.6 us (6%)
    unnamed x5, other arithmetic  118 us
    unnamed x68, local copies, waits for them, and re-layouts  48.5 us
    convert_element_type x2, local copies, waits for them, and re-layouts, unwind(): summed[WINDOW:].reshape(length, head_count, HEAD_FEATURES)  33.5 us
    all_to_all x1, waiting for transfers between devices, per_device(): lax.all_to_all(query_four, 'seq', split_axis=2, concat_axis=1, tiled=True)  28 us
    all_to_all x1, waiting for transfers between devices, per_device(): lax.all_to_all(saved_four, 'seq', split_axis=2, concat_axis=1, tiled=True)  26.7 us
    all_to_all x1, waiting for transfers between devices, per_device(): lax.all_to_all(key_cw, 'seq', split_axis=2, concat_axis=1, tiled=True)  26.6 us
    all_to_all x1, waiting for transfers between devices, per_device(): lax.all_to_all(key_nw, 'seq', split_axis=2, concat_axis=1, tiled=True)  25.9 us
    all_to_all x1, waiting for transfers between devices, per_device(): lax.all_to_all(grad_four, 'seq', split_axis=2, concat_axis=1, tiled=True)  24.3 us
  transfers between devices with their start and end apart: 13, of which 7 were waited for; matrix products, arithmetic and copies ran while one was open for 43% of the time, Pallas kernels for 0%

commit v1 on v0

v1 whole, which is shorter than its diff:
```python
import functools
import math

import jax
import jax.numpy as jnp
from jax import lax
from jax.experimental import pallas as pl
from jax.experimental.pallas import tpu as pltpu
from jax.sharding import PartitionSpec as P

F = 128
GROUP = 8
CHUNKS = 8
LEVELS = 16
BLOCKS = 32
TOK = 64
ROWS = GROUP * TOK
SCALE = 1.0 / math.sqrt(F)
LOG2E = 1.4426950408889634
MESH = pl.DeviceIdType.MESH
BF = jnp.bfloat16
F32 = jnp.float32

N, Z1, Z2, Z4, B2, S1, S3, QO, PO = range(9)


def dot(a, b, ca, cb):
    return lax.dot_general(a, b, (((ca,), (cb,)), ((), ())), preferred_element_type=F32)


def body(
    q_in, kn_in, vn_in, kc_in, vc_in, o_in, g_in, mask,
    pg_out, nk_out, nv_out, ck_out, cv_out,
    qs, gs, os, win, noisy, part, own_n, land, dqs,
    big_sem, kv_sem, in_send, in_recv, out_send, out_recv, dq_send, dq_recv,
):
    seq = lax.axis_index("seq")
    pipe = lax.axis_index("pipe")
    lev = seq // 4
    x = seq % 4
    r = x // 2
    par = x % 2
    other = 1 - par
    blk = 2 * lev + r

    mate = (lev * 4 + r * 2 + other, pipe)
    inter = (lev * 4 + 3 - x, pipe)

    def level(step):
        return (((lev + step + LEVELS) % LEVELS) * 4 + x, pipe)

    up1, up2, down1, down2 = level(1), level(2), level(-1), level(-2)
    pipe_to = (seq, (pipe + 3) % 4)
    pipe_from = (seq, (pipe + 1) % 4)

    barrier = pltpu.get_barrier_semaphore()
    for device in (mate, inter, up1, up2, down1, down2, pipe_to, pipe_from):
        pl.semaphore_signal(barrier, inc=1, device_id=device, device_id_type=MESH)

    def kv_load(c, i):
        src = (kc_in, vc_in, kn_in, vn_in)[i]
        dst = (win.at[c, 8, 0], win.at[c, 8, 1], noisy.at[c, 0, 0], noisy.at[c, 0, 1])[i]
        cols = pl.ds(pl.multiple_of(c * F, F), F)
        return pltpu.make_async_copy(src.at[0, :, cols], dst, kv_sem.at[c, i])

    def big_load(c, i):
        src = (q_in, g_in, o_in)[i]
        dst = (qs, gs, os)[i].at[c]
        cols = pl.ds(pl.multiple_of(c * GROUP * F, F), GROUP * F)
        return pltpu.make_async_copy(src.at[0, :, cols], dst, big_sem.at[c, i])

    def load_kv(c, _):
        for i in range(4):
            kv_load(c, i).start()
        return 0

    def load_big(c, _):
        for i in range(3):
            big_load(c, i).start()
        return 0

    lax.fori_loop(0, CHUNKS, load_kv, 0)
    lax.fori_loop(0, CHUNKS, load_big, 0)

    zero = jnp.zeros((2, TOK, F), BF)

    def clear(pred, ref, slots):
        @pl.when(pred)
        def _():
            def one(c, _):
                for s in slots:
                    ref[c, s] = zero
                return 0

            lax.fori_loop(0, CHUNKS, one, 0)

    clear(lev < 1, win, (2 + par, 6 + other))
    clear(lev < 2, win, (6 + par,))
    clear(lev > LEVELS - 2, land, (Z1, Z4))
    clear(lev > LEVELS - 3, land, (Z2,))

    def send_in(m, c, src, dst, device):
        return pltpu.make_async_remote_copy(
            src_ref=src, dst_ref=dst, send_sem=in_send.at[m, c], recv_sem=in_recv.at[m, c],
            device_id=device, device_id_type=MESH,
        )

    def slot(c, d, p):
        return win.at[c, 2 * d + p]

    def msg_in(m, c):
        if m == N:
            return send_in(m, c, noisy.at[c, 0], noisy.at[c, 1], mate)
        if m == Z1:
            return send_in(m, c, win.at[c, 8], slot(c, 1, par), up1)
        if m == Z2:
            return send_in(m, c, win.at[c, 8], slot(c, 3, par), up2)
        if m == Z4:
            return send_in(m, c, slot(c, 1, other), slot(c, 3, other), up1)
        if m == B2:
            return send_in(m, c, slot(c, 1, par), slot(c, 1, par), mate)
        if m == S1:
            return send_in(m, c, win.at[c, 8 - r * (6 - par)], slot(c, 0, par), inter)
        if m == S3:
            return send_in(m, c, slot(c, 1 + 2 * r, par), slot(c, 2, par), inter)
        if m == QO:
            return send_in(m, c, slot(c, 1, other), slot(c, 2 - 2 * r, other), inter)
        return send_in(m, c, slot(c, 2 - 2 * r, other), slot(c, 2 - 2 * r, other), mate)

    def msg_out(m, c):
        src = {
            N: part.at[c, 8],
            PO: part.at[c, 2 * (2 - 2 * r) + par],
            QO: part.at[c, 2 * (2 * r) + par],
            Z4: part.at[c, 6 + other],
            B2: part.at[c, 2 + other],
            S1: part.at[c, 0 + other],
            S3: part.at[c, 4 + other],
            Z1: part.at[c, 2 + par],
            Z2: part.at[c, 6 + par],
        }[m]
        device = {
            N: mate, PO: mate, B2: mate, QO: inter, S1: inter, S3: inter,
            Z4: down1, Z1: down1, Z2: down2,
        }[m]
        return pltpu.make_async_remote_copy(
            src_ref=src, dst_ref=land.at[c, m], send_sem=out_send.at[m, c], recv_sem=out_recv.at[m, c],
            device_id=device, device_id_type=MESH,
        )

    def dq_copy(c):
        cols = pl.ds(pl.multiple_of(c * GROUP * F, F), GROUP * F)
        return pltpu.make_async_remote_copy(
            src_ref=dqs.at[c], dst_ref=pg_out.at[0, :, cols], send_sem=dq_send.at[c], recv_sem=dq_recv.at[c],
            device_id=pipe_to, device_id_type=MESH,
        )

    SENDS_IN = {Z1: lev < LEVELS - 1, Z2: lev < LEVELS - 2, Z4: lev < LEVELS - 1}
    GETS_IN = {Z1: lev > 0, Z2: lev > 1, Z4: lev > 0}
    SENDS_OUT, GETS_OUT = GETS_IN, SENDS_IN

    def guarded(table, m, act):
        if m in table:
            pl.when(table[m])(act)
        else:
            act()

    def start_in(m, c):
        guarded(SENDS_IN, m, lambda: msg_in(m, c).start())

    def wait_in(m, c):
        guarded(GETS_IN, m, lambda: msg_in(m, c).wait_recv())

    def start_out(m, c):
        guarded(SENDS_OUT, m, lambda: msg_out(m, c).start())

    def wait_out(m, c):
        guarded(GETS_OUT, m, lambda: msg_out(m, c).wait_recv())

    def first_hop(c):
        for i in range(4):
            kv_load(c, i).wait()
        start_in(Z1, c)
        start_in(N, c)

        @pl.when(r == 0)
        def _():
            start_in(S1, c)

        start_in(Z2, c)

    def second_hop(c):
        wait_in(Z1, c)
        start_in(B2, c)

        @pl.when(r == 1)
        def _():
            start_in(S1, c)

        wait_in(Z2, c)
        start_in(S3, c)

    def third_hop(c):
        wait_in(B2, c)
        start_in(QO, c)
        start_in(Z4, c)
        wait_in(S1, c)
        wait_in(S3, c)
        start_in(PO, c)

    bias = []
    for d in range(4):
        flag = mask[0, blk, (blk + BLOCKS - 1 - d) % BLOCKS]
        bias.append(jnp.where((blk - 1 - d >= 0) & (flag == 1), jnp.float32(0.0), jnp.float32(-1e30)))

    def compute(c):
        wait_in(N, c)
        wait_in(QO, c)
        wait_in(Z4, c)
        wait_in(PO, c)
        for i in range(3):
            big_load(c, i).wait()

        def heads(ref):
            return jnp.concatenate([ref[c, :, h * F : (h + 1) * F] for h in range(GROUP)], axis=0)

        q = heads(qs)
        g = heads(gs)
        o = heads(os)

        def pairs(i):
            out = [noisy[c, :, i].reshape(2 * TOK, F)]
            for d in range(4):
                out.append(jnp.concatenate([win[c, 2 * d, i], win[c, 2 * d + 1, i]], axis=0))
            return out

        keys = pairs(0)
        values = pairs(1)
        prod = g.astype(F32) * o.astype(F32)
        high = prod.astype(BF)
        low = (prod - high.astype(F32)).astype(BF)
        ones = jnp.ones((16, F), BF)
        delta = (dot(ones, high, 1, 1) + dot(ones, low, 1, 1))[0:1]

        const = SCALE * LOG2E
        scores = [dot(k, q, 1, 1) for k in keys]
        tops = [s.max(axis=0, keepdims=True) * const for s in scores]
        top = tops[0]
        for d in range(4):
            top = jnp.maximum(top, tops[d + 1] + bias[d])
        exps = []
        total = jnp.zeros((1, ROWS), F32)
        for d, s in enumerate(scores):
            shift = top if d == 0 else top - bias[d - 1]
            e = jnp.exp2(s * const - shift)
            total = total + e.sum(axis=0, keepdims=True)
            exps.append(e)
        inv = 1.0 / total
        dq = jnp.zeros((F, ROWS), F32)
        for d in range(5):
            p = exps[d] * inv
            dp = dot(values[d], g, 1, 1)
            ds = (p * (dp - delta)).astype(BF)
            dq = dq + dot(keys[d], ds, 0, 0)
            dk = dot(ds, q, 1, 0) * SCALE
            dv = dot(p.astype(BF), g, 1, 0)
            if d == 0:
                own_n[c, 0] = dk[:TOK]
                own_n[c, 1] = dv[:TOK]
                part[c, 8, 0] = dk[TOK:].astype(BF)
                part[c, 8, 1] = dv[TOK:].astype(BF)
            else:
                s0 = 2 * (d - 1)
                part[c, s0, 0] = dk[:TOK].astype(BF)
                part[c, s0, 1] = dv[:TOK].astype(BF)
                part[c, s0 + 1, 0] = dk[TOK:].astype(BF)
                part[c, s0 + 1, 1] = dv[TOK:].astype(BF)
        dq = (dq.T * SCALE).astype(BF)
        for h in range(GROUP):
            dqs[c, :, h * F : (h + 1) * F] = dq[h * TOK : (h + 1) * TOK]
        start_out(PO, c)
        start_out(QO, c)
        start_out(Z4, c)
        start_out(N, c)
        dq_copy(c).start()

    def wide(ref, *index):
        return ref[index].astype(F32)

    def second_out(c):
        for m in (PO, QO, Z4):
            wait_out(m, c)
        part[c, 2 + other] = (wide(part, c, 2 + other) + wide(land, c, QO) + wide(land, c, Z4)).astype(BF)
        s = 2 * (2 - 2 * r) + other
        part[c, s] = (wide(part, c, s) + wide(land, c, PO)).astype(BF)
        start_out(S1, c)
        start_out(S3, c)
        start_out(B2, c)

    def third_out(c):
        for m in (S1, S3, B2):
            wait_out(m, c)
        first = wide(land, c, S1)
        third = wide(land, c, S3)
        part[c, 2 + par] = (
            wide(part, c, 2 + par) + wide(land, c, B2) + jnp.where(r == 1, first, third)
        ).astype(BF)
        start_out(Z1, c)
        part[c, 6 + par] = (wide(part, c, 6 + par) + jnp.where(r == 1, third, 0.0)).astype(BF)
        start_out(Z2, c)

    def last_out(c):
        for m in (N, Z1, Z2):
            wait_out(m, c)
        cols = pl.ds(pl.multiple_of(c * F, F), F)
        clean = wide(land, c, Z1) + wide(land, c, Z2) + jnp.where(r == 0, wide(land, c, S1), 0.0)
        ck_out[0, :, cols] = clean[0].astype(BF)
        cv_out[0, :, cols] = clean[1].astype(BF)
        dirty = own_n[c] + wide(land, c, N)
        nk_out[0, :, cols] = dirty[0].astype(BF)
        nv_out[0, :, cols] = dirty[1].astype(BF)

    pl.semaphore_wait(barrier, 8)
    AHEAD = 2
    for c in range(AHEAD):
        first_hop(c)

    stages = (second_hop, third_hop, compute, second_out, third_out, last_out)

    def step(k, _):
        pl.when(k + AHEAD < CHUNKS)(lambda: first_hop(k + AHEAD))
        for lag, stage in enumerate(stages):
            pl.when((k >= lag) & (k - lag < CHUNKS))(functools.partial(stage, k - lag))
        return 0

    lax.fori_loop(0, CHUNKS + len(stages) - 1, step, 0)

    def drain(c, _):
        dq_copy(c).wait()
        for m in range(9):
            guarded(SENDS_IN, m, lambda: msg_in(m, c).wait_send())
            guarded(SENDS_OUT, m, lambda: msg_out(m, c).wait_send())
        return 0

    lax.fori_loop(0, CHUNKS, drain, 0)


def per_device(noisy_q, noisy_k, noisy_v, clean_k, clean_v, noisy_o, out_grad, block_mask):
    kv = jax.ShapeDtypeStruct(noisy_k.shape, BF)
    hbm = pl.BlockSpec(memory_space=pl.ANY)
    vmem = pl.BlockSpec(memory_space=pltpu.VMEM)
    dma = pltpu.SemaphoreType.DMA
    wide = (CHUNKS, TOK, GROUP * F)
    return pl.pallas_call(
        body,
        out_shape=(jax.ShapeDtypeStruct(noisy_q.shape, BF), kv, kv, kv, kv),
        in_specs=[hbm] * 7 + [pl.BlockSpec(memory_space=pltpu.SMEM)],
        out_specs=(hbm, vmem, vmem, vmem, vmem),
        scratch_shapes=[
            pltpu.VMEM(wide, BF),
            pltpu.VMEM(wide, BF),
            pltpu.VMEM(wide, BF),
            pltpu.VMEM((CHUNKS, 9, 2, TOK, F), BF),
            pltpu.VMEM((CHUNKS, 2, 2, TOK, F), BF),
            pltpu.VMEM((CHUNKS, 9, 2, TOK, F), BF),
            pltpu.VMEM((CHUNKS, 2, TOK, F), F32),
            pltpu.VMEM((CHUNKS, 9, 2, TOK, F), BF),
            pltpu.VMEM(wide, BF),
            dma((CHUNKS, 3)),
            dma((CHUNKS, 4)),
            dma((9, CHUNKS)),
            dma((9, CHUNKS)),
            dma((9, CHUNKS)),
            dma((9, CHUNKS)),
            dma((CHUNKS,)),
            dma((CHUNKS,)),
        ],
        compiler_params=pltpu.CompilerParams(
            collective_id=0, has_side_effects=True, vmem_limit_bytes=48 << 20
        ),
        cost_estimate=pl.CostEstimate(flops=3400000000, bytes_accessed=6 << 20, transcendentals=2700000),
    )(noisy_q, noisy_k, noisy_v, clean_k, clean_v, noisy_o, out_grad, block_mask)


def solution(mesh):
    three = P("pipe", "seq", None)
    return jax.shard_map(
        per_device, mesh=mesh, in_specs=(three,) * 7 + (P("pipe", None, None),), out_specs=(three,) * 5,
        check_vma=False,
    )
```

time: 584 us -> 79 us (0.14); the launches traced: 572 us -> 78.7 us
  waiting for transfers between devices: 158 us -> 0 us
  other arithmetic: 135 us -> 0 us
  local copies, waits for them, and re-layouts: 134 us -> 11.6 us
  starting transfers between devices: 106 us -> 0 us
  Pallas kernels: 0 us -> 66.4 us
  matrix products: 37.6 us -> 0 us
    all_to_all x12 -> x0, waiting for transfers between devices: 158 us -> none  [the longest x1 28 us: per_device(): lax.all_to_all(query_four, 'seq', split_axis=2, concat_axis=1, tiled=True)]
    unnamed x5 -> x0, other arithmetic: 118 us -> none
    all_to_all x12 -> x0, starting transfers between devices: 106 us -> none  [the longest x1 12.7 us: per_device(): lax.all_to_all(query_four, 'seq', split_axis=2, concat_axis=1, tiled=True)]
    pallas_call x0 -> x1, Pallas kernels: none -> 66.4 us  [per_device(): pl.pallas_call(body, out_shape=(jax.ShapeDtypeStruct(noisy_q.shape, BF),...]
    dot_general x10 -> x0, matrix products: 37.6 us -> none  [the longest x1 7.54 us: attend_heads(): jnp.einsum('bhqk,bqhd->bkhd', probs_c.astype(jnp.bfloat16), grad_blk, pre...]
    unnamed x68 -> x21, local copies, waits for them, and re-layouts: 48.5 us -> 11.6 us
    convert_element_type x3 -> x0, local copies, waits for them, and re-layouts: 35.8 us -> none  [the longest x2 33.5 us: unwind(): summed[WINDOW:].reshape(length, head_count, HEAD_FEATURES)]
    another operation x3 -> x0, local copies, waits for them, and re-layouts: 25.4 us -> none  [the longest x1 16.7 us: attend_heads(): dvalue_noisy[None]]
  transfers between devices with their start and end apart: 13 -> 0, of which waited for: 7 -> 0; matrix products, arithmetic and copies ran while one was open for 43% -> 0% of each run, Pallas kernels for 0% -> 0%
where the time goes in v1:
time: 79 us; the launch traced here: 78.7 us
  Pallas kernels  66.4 us (84%)
  local copies, waits for them, and re-layouts  11.6 us (15%)
    pallas_call x1, Pallas kernels, per_device(): pl.pallas_call(body, out_shape=(jax.ShapeDtypeStruct(noisy_q.shape, BF),...  66.4 us
    unnamed x21, local copies, waits for them, and re-layouts  11.6 us

profile of v1, /device:TPU:16, one launch (start us, length us, event | category | flops | bytes accessed | tf_op | source)
XLA Modules:
  0.0 78.7 jit_solution(15690529877494219742)
XLA Ops:
  0.6 0.0 copy-start
  0.6 1.2 %copy-done = bf16[1,64,8192]{2,1,0:T(8,128)(2,1)S(1)} copy-done((bf16[1,64,8192]{2,1,0:T(8,128)(2,1)S(1)}, bf16[1,64,8192]{2,1,0:T(8,128)(2,1)}, u32[]{:S(2)}) %copy-start) | copy-done | bytes 1048600
  1.9 0.0 copy-start.1
  1.9 1.2 %copy-done.1 = bf16[1,64,8192]{2,1,0:T(8,128)(2,1)S(1)} copy-done((bf16[1,64,8192]{2,1,0:T(8,128)(2,1)S(1)}, bf16[1,64,8192]{2,1,0:T(8,128)(2,1)}, u32[]{:S(2)}) %copy-start.1) | copy-done | bytes 1048600
  3.1 0.0 copy-start.2
  3.1 1.2 %copy-done.2 = bf16[1,64,8192]{2,1,0:T(8,128)(2,1)S(1)} copy-done((bf16[1,64,8192]{2,1,0:T(8,128)(2,1)S(1)}, bf16[1,64,8192]{2,1,0:T(8,128)(2,1)}, u32[]{:S(2)}) %copy-start.2) | copy-done | bytes 1048600
  4.3 0.0 copy-start.3
  4.3 0.9 %copy-done.3 = bf16[1,64,1024]{2,1,0:T(8,128)(2,1)S(1)} copy-done((bf16[1,64,1024]{2,1,0:T(8,128)(2,1)S(1)}, bf16[1,64,1024]{2,1,0:T(8,128)(2,1)}, u32[]{:S(2)}) %copy-start.3) | copy-done | bytes 131096
  5.2 0.0 copy-start.4
  5.2 0.9 %copy-done.4 = bf16[1,64,1024]{2,1,0:T(8,128)(2,1)S(1)} copy-done((bf16[1,64,1024]{2,1,0:T(8,128)(2,1)S(1)}, bf16[1,64,1024]{2,1,0:T(8,128)(2,1)}, u32[]{:S(2)}) %copy-start.4) | copy-done | bytes 131096
  6.1 0.0 copy-start.5
  6.1 0.9 %copy-done.5 = bf16[1,64,1024]{2,1,0:T(8,128)(2,1)S(1)} copy-done((bf16[1,64,1024]{2,1,0:T(8,128)(2,1)S(1)}, bf16[1,64,1024]{2,1,0:T(8,128)(2,1)}, u32[]{:S(2)}) %copy-start.5) | copy-done | bytes 131096
  7.0 0.0 copy-start.6
  7.0 0.9 %copy-done.6 = bf16[1,64,1024]{2,1,0:T(8,128)(2,1)S(1)} copy-done((bf16[1,64,1024]{2,1,0:T(8,128)(2,1)S(1)}, bf16[1,64,1024]{2,1,0:T(8,128)(2,1)}, u32[]{:S(2)}) %copy-start.6) | copy-done | bytes 131096
  7.9 0.0 copy-start.7
  7.9 0.7 copy-done.7
  8.6 66.4 %shard_map.119 = (bf16[1,64,8192]{2,1,0:T(8,128)(2,1)S(1)}, bf16[1,64,1024]{2,1,0:T(8,128)(2,1)S(1)}, bf16[1,64,1024]{2,1,0:T(8,128)(2,1)S(1)}, bf16[1,64,1024]{2,1,0:T(8,128)(2,1)S(1)}, bf16[1,64,1024]{2,1,0:T(8,128)(2,1)S(1)}) custom-call(bf16[1,64,8192]{2,1,0:T(8,128)(2,1)S(1)} %copy-done, bf16[1,64,1024]{2,1,0:T(8,128)(2,1)S(1)} %copy-done.3, ...), custom_call_target="tpu_custom_call" | custom-call | flops 3400000000 | bytes 6291456 | tf_op jit(solution)/shard_map/pallas_call | solution.py:354
  75.1 1.0 %copy.18 = bf16[1,64,8192]{2,1,0:T(8,128)(2,1)} copy(bf16[1,64,8192]{2,1,0:T(8,128)(2,1)S(1)} %get-tuple-element.10) | data formatting | bytes 2097152
  76.1 0.7 copy.19
  76.7 0.7 copy.20
  77.4 0.7 copy.21
  78.0 0.7 copy.22
Async XLA Ops:
  0.6 1.2 %copy-start = (bf16[1,64,8192]{2,1,0:T(8,128)(2,1)S(1)}, bf16[1,64,8192]{2,1,0:T(8,128)(2,1)}, u32[]{:S(2)}) copy-start(bf16[1,64,8192]{2,1,0:T(8,128)(2,1)} %q_in.1) | copy-start | bytes 3145732
  1.9 1.2 %copy-start.1 = (bf16[1,64,8192]{2,1,0:T(8,128)(2,1)S(1)}, bf16[1,64,8192]{2,1,0:T(8,128)(2,1)}, u32[]{:S(2)}) copy-start(bf16[1,64,8192]{2,1,0:T(8,128)(2,1)} %o_in.1) | copy-start | bytes 3145732
  3.1 1.2 %copy-start.2 = (bf16[1,64,8192]{2,1,0:T(8,128)(2,1)S(1)}, bf16[1,64,8192]{2,1,0:T(8,128)(2,1)}, u32[]{:S(2)}) copy-start(bf16[1,64,8192]{2,1,0:T(8,128)(2,1)} %g_in.1) | copy-start | bytes 3145732
  4.3 0.9 %copy-start.3 = (bf16[1,64,1024]{2,1,0:T(8,128)(2,1)S(1)}, bf16[1,64,1024]{2,1,0:T(8,128)(2,1)}, u32[]{:S(2)}) copy-start(bf16[1,64,1024]{2,1,0:T(8,128)(2,1)} %kn_in.1) | copy-start | bytes 393220
  5.2 0.9 %copy-start.4 = (bf16[1,64,1024]{2,1,0:T(8,128)(2,1)S(1)}, bf16[1,64,1024]{2,1,0:T(8,128)(2,1)}, u32[]{:S(2)}) copy-start(bf16[1,64,1024]{2,1,0:T(8,128)(2,1)} %vn_in.1) | copy-start | bytes 393220
  6.1 0.9 %copy-start.5 = (bf16[1,64,1024]{2,1,0:T(8,128)(2,1)S(1)}, bf16[1,64,1024]{2,1,0:T(8,128)(2,1)}, u32[]{:S(2)}) copy-start(bf16[1,64,1024]{2,1,0:T(8,128)(2,1)} %kc_in.1) | copy-start | bytes 393220
  7.0 0.9 %copy-start.6 = (bf16[1,64,1024]{2,1,0:T(8,128)(2,1)S(1)}, bf16[1,64,1024]{2,1,0:T(8,128)(2,1)}, u32[]{:S(2)}) copy-start(bf16[1,64,1024]{2,1,0:T(8,128)(2,1)} %vc_in.1) | copy-start | bytes 393220
  7.9 0.7 copy-start.7

commit v2 on v1

--- a/solution.py
+++ b/solution.py
@@ -29,9 +29,9 @@
 
 
 def body(
-    q_in, kn_in, vn_in, kc_in, vc_in, o_in, g_in, mask,
+    q_in, kn_in, vn_in, kc_in, vc_in, o_in, g_in, mask_in,
     pg_out, nk_out, nv_out, ck_out, cv_out,
-    qs, gs, os, win, noisy, part, own_n, land, dqs,
+    mask, mask_sem, qs, gs, os, win, noisy, part, own_n, land, dqs,
     big_sem, kv_sem, in_send, in_recv, out_send, out_recv, dq_send, dq_recv,
 ):
     seq = lax.axis_index("seq")
@@ -79,6 +79,8 @@
             big_load(c, i).start()
         return 0
 
+    mask_load = pltpu.make_async_copy(mask_in, mask, mask_sem)
+    mask_load.start()
     lax.fori_loop(0, CHUNKS, load_kv, 0)
     lax.fori_loop(0, CHUNKS, load_big, 0)
 
@@ -208,6 +210,7 @@
         wait_in(S3, c)
         start_in(PO, c)
 
+    mask_load.wait()
     bias = []
     for d in range(4):
         flag = mask[0, blk, (blk + BLOCKS - 1 - d) % BLOCKS]
@@ -321,19 +324,25 @@
         nv_out[0, :, cols] = dirty[1].astype(BF)
 
     pl.semaphore_wait(barrier, 8)
-    AHEAD = 2
-    for c in range(AHEAD):
+    for c in range(2):
         first_hop(c)
 
-    stages = (second_hop, third_hop, compute, second_out, third_out, last_out)
+    def stage(k, fn, lag, rate):
+        for b in range(rate):
+            c = rate * (k - lag) + b
+            pl.when((c >= 0) & (c < CHUNKS))(functools.partial(fn, c))
 
     def step(k, _):
-        pl.when(k + AHEAD < CHUNKS)(lambda: first_hop(k + AHEAD))
-        for lag, stage in enumerate(stages):
-            pl.when((k >= lag) & (k - lag < CHUNKS))(functools.partial(stage, k - lag))
+        pl.when(k + 2 < CHUNKS)(lambda: first_hop(k + 2))
+        stage(k, second_hop, 0, 1)
+        stage(k, third_hop, 2, 1)
+        stage(k, compute, 4, 1)
+        stage(k, second_out, 6, 1)
+        stage(k, third_out, 8, 1)
+        stage(k, last_out, 10, 1)
         return 0
 
-    lax.fori_loop(0, CHUNKS + len(stages) - 1, step, 0)
+    lax.fori_loop(0, CHUNKS + 10, step, 0)
 
     def drain(c, _):
         dq_copy(c).wait()
@@ -345,18 +354,29 @@
     lax.fori_loop(0, CHUNKS, drain, 0)
 
 
-def per_device(noisy_q, noisy_k, noisy_v, clean_k, clean_v, noisy_o, out_grad, block_mask):
+def finish(*refs):
+    copies = [pltpu.make_async_copy(refs[i], refs[5 + i], refs[10].at[i]) for i in range(5)]
+    for copy in copies:
+        copy.start()
+    for copy in copies:
+        copy.wait()
+
+
+def per_device(*args):
+    noisy_q, noisy_k = args[:2]
     kv = jax.ShapeDtypeStruct(noisy_k.shape, BF)
-    hbm = pl.BlockSpec(memory_space=pl.ANY)
+    hbm = pl.BlockSpec(memory_space=pltpu.HBM)
     vmem = pl.BlockSpec(memory_space=pltpu.VMEM)
     dma = pltpu.SemaphoreType.DMA
     wide = (CHUNKS, TOK, GROUP * F)
-    return pl.pallas_call(
+    outs = pl.pallas_call(
         body,
-        out_shape=(jax.ShapeDtypeStruct(noisy_q.shape, BF), kv, kv, kv, kv),
-        in_specs=[hbm] * 7 + [pl.BlockSpec(memory_space=pltpu.SMEM)],
-        out_specs=(hbm, vmem, vmem, vmem, vmem),
+        out_shape=(pltpu.VMEM(noisy_q.shape, BF),) + (pltpu.VMEM(noisy_k.shape, BF),) * 4,
+        in_specs=[hbm] * 8,
+        out_specs=(vmem,) * 5,
         scratch_shapes=[
+            pltpu.SMEM((1, BLOCKS, BLOCKS), jnp.int32),
+            dma(()),
             pltpu.VMEM(wide, BF),
             pltpu.VMEM(wide, BF),
             pltpu.VMEM(wide, BF),
@@ -376,10 +396,18 @@
             dma((CHUNKS,)),
         ],
         compiler_params=pltpu.CompilerParams(
-            collective_id=0, has_side_effects=True, vmem_limit_bytes=48 << 20
+            collective_id=0, has_side_effects=True, vmem_limit_bytes=40 << 20
         ),
         cost_estimate=pl.CostEstimate(flops=3400000000, bytes_accessed=6 << 20, transcendentals=2700000),
-    )(noisy_q, noisy_k, noisy_v, clean_k, clean_v, noisy_o, out_grad, block_mask)
+    )(*[pltpu.with_memory_space_constraint(a, pltpu.HBM) for a in args])
+    return pl.pallas_call(
+        finish,
+        out_shape=(jax.ShapeDtypeStruct(noisy_q.shape, BF), kv, kv, kv, kv),
+        in_specs=[vmem] * 5,
+        out_specs=(hbm,) * 5,
+        scratch_shapes=[dma((5,))],
+        compiler_params=pltpu.CompilerParams(vmem_limit_bytes=8 << 20),
+    )(*outs)
 
 
 def solution(mesh):

time: 79 us -> 62.8 us (0.79)
  local copies, waits for them, and re-layouts: 11.6 us -> 0 us
  Pallas kernels: 66.4 us -> 61.4 us
    unnamed x21 -> x0, local copies, waits for them, and re-layouts: 11.6 us -> none
    pallas_call x1 -> x2, Pallas kernels: 66.4 us -> 61.4 us  [the longest x1 60.2 us: per_device(): pl.pallas_call(body, out_shape=(pltpu.VMEM(noisy_q.shape, BF),) + (pltpu....]
where the time goes in v2:
time: 62.8 us; the launch traced here: 62.1 us
  Pallas kernels  61.4 us (98%)
  between operations  0.64 us (1%)
    pallas_call x1, Pallas kernels, per_device(): pl.pallas_call(body, out_shape=(pltpu.VMEM(noisy_q.shape, BF),) + (pltpu....  60.2 us

profile of v2, /device:TPU:16, one launch (start us, length us, event | category | flops | bytes accessed | tf_op | source)
XLA Modules:
  0.0 62.1 jit_solution(5001525710892117550)
XLA Ops:
  0.6 60.2 %shard_map.119 = (bf16[1,64,8192]{2,1,0:T(8,128)(2,1)S(1)}, bf16[1,64,1024]{2,1,0:T(8,128)(2,1)S(1)}, bf16[1,64,1024]{2,1,0:T(8,128)(2,1)S(1)}, bf16[1,64,1024]{2,1,0:T(8,128)(2,1)S(1)}, bf16[1,64,1024]{2,1,0:T(8,128)(2,1)S(1)}) custom-call(bf16[1,64,8192]{2,1,0:T(8,128)(2,1)} %q_in.1, bf16[1,64,1024]{2,1,0:T(8,128)(2,1)} %kn_in.1, ...), custom_call_target="tpu_custom_call" | custom-call | flops 3400000000 | bytes 6291456 | tf_op jit(solution)/shard_map/pallas_call | solution.py:372
  60.9 1.2 %shard_map.120 = (bf16[1,64,8192]{2,1,0:T(8,128)(2,1)}, bf16[1,64,1024]{2,1,0:T(8,128)(2,1)}, bf16[1,64,1024]{2,1,0:T(8,128)(2,1)}, bf16[1,64,1024]{2,1,0:T(8,128)(2,1)}, bf16[1,64,1024]{2,1,0:T(8,128)(2,1)}) custom-call(bf16[1,64,8192]{2,1,0:T(8,128)(2,1)S(1)} %get-tuple-element.10.refs_0_, bf16[1,64,1024]{2,1,0:T(8,128)(2,1)S(1)} %get-tuple-element.11.refs_1_, ...), custom_call_target="tpu_custom_call" | custom-call | tf_op jit(solution)/shard_map/pallas_call | solution.py:403

commit v3 on v2

--- a/solution.py
+++ b/solution.py
@@ -81,8 +81,9 @@
 
     mask_load = pltpu.make_async_copy(mask_in, mask, mask_sem)
     mask_load.start()
-    lax.fori_loop(0, CHUNKS, load_kv, 0)
-    lax.fori_loop(0, CHUNKS, load_big, 0)
+    AHEAD = 2
+    for c in range(AHEAD):
+        load_kv(c, 0)
 
     zero = jnp.zeros((2, TOK, F), BF)
 
@@ -260,7 +261,7 @@
             exps.append(e)
         inv = 1.0 / total
         dq = jnp.zeros((F, ROWS), F32)
-        for d in range(5):
+        for d in (1, 3, 4, 0, 2):
             p = exps[d] * inv
             dp = dot(values[d], g, 1, 1)
             ds = (p * (dp - delta)).astype(BF)
@@ -278,26 +279,34 @@
                 part[c, s0, 1] = dv[:TOK].astype(BF)
                 part[c, s0 + 1, 0] = dk[TOK:].astype(BF)
                 part[c, s0 + 1, 1] = dv[TOK:].astype(BF)
+            if d == 3:
+                start_out(PO, c)
+                start_out(QO, c)
+                pl.when(r == 0)(lambda: start_out(S1, c))
+                pl.when(r == 1)(lambda: start_out(S3, c))
+            elif d == 4:
+                start_out(Z4, c)
+                pl.when(r == 0)(lambda: start_out(Z2, c))
+            elif d == 0:
+                start_out(N, c)
         dq = (dq.T * SCALE).astype(BF)
         for h in range(GROUP):
             dqs[c, :, h * F : (h + 1) * F] = dq[h * TOK : (h + 1) * TOK]
-        start_out(PO, c)
-        start_out(QO, c)
-        start_out(Z4, c)
-        start_out(N, c)
         dq_copy(c).start()
 
     def wide(ref, *index):
         return ref[index].astype(F32)
 
     def second_out(c):
+        for m in range(9):
+            guarded(SENDS_IN, m, lambda: msg_in(m, c).wait_send())
         for m in (PO, QO, Z4):
             wait_out(m, c)
         part[c, 2 + other] = (wide(part, c, 2 + other) + wide(land, c, QO) + wide(land, c, Z4)).astype(BF)
         s = 2 * (2 - 2 * r) + other
         part[c, s] = (wide(part, c, s) + wide(land, c, PO)).astype(BF)
-        start_out(S1, c)
-        start_out(S3, c)
+        pl.when(r == 0)(lambda: start_out(S3, c))
+        pl.when(r == 1)(lambda: start_out(S1, c))
         start_out(B2, c)
 
     def third_out(c):
@@ -309,8 +318,11 @@
             wide(part, c, 2 + par) + wide(land, c, B2) + jnp.where(r == 1, first, third)
         ).astype(BF)
         start_out(Z1, c)
-        part[c, 6 + par] = (wide(part, c, 6 + par) + jnp.where(r == 1, third, 0.0)).astype(BF)
-        start_out(Z2, c)
+
+        @pl.when(r == 1)
+        def _():
+            part[c, 6 + par] = (wide(part, c, 6 + par) + third).astype(BF)
+            start_out(Z2, c)
 
     def last_out(c):
         for m in (N, Z1, Z2):
@@ -322,10 +334,15 @@
         dirty = own_n[c] + wide(land, c, N)
         nk_out[0, :, cols] = dirty[0].astype(BF)
         nv_out[0, :, cols] = dirty[1].astype(BF)
+        dq_copy(c).wait()
+        for m in range(9):
+            guarded(SENDS_OUT, m, lambda: msg_out(m, c).wait_send())
 
     pl.semaphore_wait(barrier, 8)
-    for c in range(2):
+    for c in range(AHEAD):
         first_hop(c)
+    lax.fori_loop(AHEAD, CHUNKS, load_kv, 0)
+    lax.fori_loop(0, CHUNKS, load_big, 0)
 
     def stage(k, fn, lag, rate):
         for b in range(rate):
@@ -333,7 +350,7 @@
             pl.when((c >= 0) & (c < CHUNKS))(functools.partial(fn, c))
 
     def step(k, _):
-        pl.when(k + 2 < CHUNKS)(lambda: first_hop(k + 2))
+        pl.when(k + AHEAD < CHUNKS)(lambda: first_hop(k + AHEAD))
         stage(k, second_hop, 0, 1)
         stage(k, third_hop, 2, 1)
         stage(k, compute, 4, 1)
@@ -343,15 +360,6 @@
         return 0
 
     lax.fori_loop(0, CHUNKS + 10, step, 0)
-
-    def drain(c, _):
-        dq_copy(c).wait()
-        for m in range(9):
-            guarded(SENDS_IN, m, lambda: msg_in(m, c).wait_send())
-            guarded(SENDS_OUT, m, lambda: msg_out(m, c).wait_send())
-        return 0
-
-    lax.fori_loop(0, CHUNKS, drain, 0)
 
 
 def finish(*refs):

time: 62.8 us -> 60.2 us (0.959)
  Pallas kernels: 61.4 us -> 59.2 us
    pallas_call x1, Pallas kernels: 60.2 us -> 58.1 us  [per_device(): pl.pallas_call(body, out_shape=(pltpu.VMEM(noisy_q.shape, BF),) + (pltpu....]
where the time goes in v3:
time: 60.2 us; the launch traced here: 59.9 us
  Pallas kernels  59.2 us (98%)
  between operations  0.64 us (1%)
    pallas_call x1, Pallas kernels, per_device(): pl.pallas_call(body, out_shape=(pltpu.VMEM(noisy_q.shape, BF),) + (pltpu....  58.1 us

profile of v3, /device:TPU:16, one launch (start us, length us, event | category | flops | bytes accessed | tf_op | source)
XLA Modules:
  0.0 59.9 jit_solution(8615817638894508305)
XLA Ops:
  0.6 58.1 %shard_map.119 = (bf16[1,64,8192]{2,1,0:T(8,128)(2,1)S(1)}, bf16[1,64,1024]{2,1,0:T(8,128)(2,1)S(1)}, bf16[1,64,1024]{2,1,0:T(8,128)(2,1)S(1)}, bf16[1,64,1024]{2,1,0:T(8,128)(2,1)S(1)}, bf16[1,64,1024]{2,1,0:T(8,128)(2,1)S(1)}) custom-call(bf16[1,64,8192]{2,1,0:T(8,128)(2,1)} %q_in.1, bf16[1,64,1024]{2,1,0:T(8,128)(2,1)} %kn_in.1, ...), custom_call_target="tpu_custom_call" | custom-call | flops 3400000000 | bytes 6291456 | tf_op jit(solution)/shard_map/pallas_call | solution.py:380
  58.7 1.2 %shard_map.120 = (bf16[1,64,8192]{2,1,0:T(8,128)(2,1)}, bf16[1,64,1024]{2,1,0:T(8,128)(2,1)}, bf16[1,64,1024]{2,1,0:T(8,128)(2,1)}, bf16[1,64,1024]{2,1,0:T(8,128)(2,1)}, bf16[1,64,1024]{2,1,0:T(8,128)(2,1)}) custom-call(bf16[1,64,8192]{2,1,0:T(8,128)(2,1)S(1)} %get-tuple-element.10.refs_0_, bf16[1,64,1024]{2,1,0:T(8,128)(2,1)S(1)} %get-tuple-element.11.refs_1_, ...), custom_call_target="tpu_custom_call" | custom-call | tf_op jit(solution)/shard_map/pallas_call | solution.py:411

commit v4 on v3

--- a/solution.py
+++ b/solution.py
@@ -260,12 +260,12 @@
             total = total + e.sum(axis=0, keepdims=True)
             exps.append(e)
         inv = 1.0 / total
-        dq = jnp.zeros((F, ROWS), F32)
+        grads = {}
         for d in (1, 3, 4, 0, 2):
             p = exps[d] * inv
             dp = dot(values[d], g, 1, 1)
             ds = (p * (dp - delta)).astype(BF)
-            dq = dq + dot(keys[d], ds, 0, 0)
+            grads[d] = ds
             dk = dot(ds, q, 1, 0) * SCALE
             dv = dot(p.astype(BF), g, 1, 0)
             if d == 0:
@@ -289,6 +289,7 @@
                 pl.when(r == 0)(lambda: start_out(Z2, c))
             elif d == 0:
                 start_out(N, c)
+        dq = sum(dot(keys[d], grads[d], 0, 0) for d in range(5))
         dq = (dq.T * SCALE).astype(BF)
         for h in range(GROUP):
             dqs[c, :, h * F : (h + 1) * F] = dq[h * TOK : (h + 1) * TOK]

time: 60.2 us -> 59.9 us (level)
  no operation moved by 1% of the time
where the time goes in v4:
time: 59.9 us; the launch traced here: 59.5 us
  Pallas kernels  58.9 us (98%)
  between operations  0.64 us (1%)
    pallas_call x1, Pallas kernels, per_device(): pl.pallas_call(body, out_shape=(pltpu.VMEM(noisy_q.shape, BF),) + (pltpu....  57.7 us

profile of v4, /device:TPU:16, one launch (start us, length us, event | category | flops | bytes accessed | tf_op | source)
XLA Modules:
  0.0 59.5 jit_solution(5851933730750428827)
XLA Ops:
  0.6 57.7 %shard_map.119 = (bf16[1,64,8192]{2,1,0:T(8,128)(2,1)S(1)}, bf16[1,64,1024]{2,1,0:T(8,128)(2,1)S(1)}, bf16[1,64,1024]{2,1,0:T(8,128)(2,1)S(1)}, bf16[1,64,1024]{2,1,0:T(8,128)(2,1)S(1)}, bf16[1,64,1024]{2,1,0:T(8,128)(2,1)S(1)}) custom-call(bf16[1,64,8192]{2,1,0:T(8,128)(2,1)} %q_in.1, bf16[1,64,1024]{2,1,0:T(8,128)(2,1)} %kn_in.1, ...), custom_call_target="tpu_custom_call" | custom-call | flops 3400000000 | bytes 6291456 | tf_op jit(solution)/shard_map/pallas_call | solution.py:381
  58.4 1.2 %shard_map.120 = (bf16[1,64,8192]{2,1,0:T(8,128)(2,1)}, bf16[1,64,1024]{2,1,0:T(8,128)(2,1)}, bf16[1,64,1024]{2,1,0:T(8,128)(2,1)}, bf16[1,64,1024]{2,1,0:T(8,128)(2,1)}, bf16[1,64,1024]{2,1,0:T(8,128)(2,1)}) custom-call(bf16[1,64,8192]{2,1,0:T(8,128)(2,1)S(1)} %get-tuple-element.10.refs_0_, bf16[1,64,1024]{2,1,0:T(8,128)(2,1)S(1)} %get-tuple-element.11.refs_1_, ...), custom_call_target="tpu_custom_call" | custom-call | tf_op jit(solution)/shard_map/pallas_call | solution.py:412
